TPU v7x, 32 devices: a whole 2x2x4 slice. The times are simulated.
32 devices in a mesh: parts: 2 (over x), node: 16 (over z, y, core).
Axes of the slice: x: 2, y: 2, z: 4, core: 2. Of those that a mesh axis runs over, the one named last changes fastest.
Arguments:
- node_field: float32 [64, 8192], P(None, ('parts', 'node')), parts along dimension 1, may hold values from -8 to 8
- first_messages: float32 [64, 65536], P(None, ('parts', 'node')), parts along dimension 1, may hold values from 0.05 to 1
- affinity: float32 [64, 64], replicated, may hold values from 1 to 30, as said below
- group_share: float32 [64], replicated, may hold values from 0.005 to 0.05
- dst_node: int32 [65536], P(('parts', 'node')), parts along dimension 0, may hold values from 0 to 256, as said below
- send_slots: int32 [32768], P(('parts', 'node')), parts along dimension 0, may hold values from 0 to 2047, as said below
- source_slot: int32 [65536], P(('parts', 'node')), parts along dimension 0, may hold values from 0 to 3071, as said below
Outputs:
- marginals: float32 [64, 8192], P(None, ('parts', 'node')), parts along dimension 1
- cavity_terms: float32 [64, 65536], P(None, ('parts', 'node')), parts along dimension 1
There are 2 independent parts, one for each index of `parts`. A program takes and returns all parts, laid end to end along the dimension named above; an argument that names none is the same for every part. Nothing has to cross between parts.
Inputs may be any that keep to these rules, and one draw needn't show every extreme that they name: `dst_node`: on each device the 2048 slots list the live edges by receiving node, sorted, then the padding marked 256; every device has a node with 96 or more incoming edges. `send_slots`: entry b * 64 + t of a device's 16 * 64 entries is the slot whose new message travels to device b into place t; at most 64 of the entries for one peer are live slots, and every device has exactly 64 live ones for one peer, also in the other direction. `source_slot`: each live slot names the live slot of its reverse edge, among this device's 2048 slots or among the 1024 places received; a padding slot names itself. `affinity`: Symmetric.
All inputs are finite; a program needn't handle non-finite values.
Results may differ from a plain program's by a relative error of at most 0.0003.
Values sent between devices are 32-bit elements; how exact they have to be, the bound alone decides.
A program may use at most 64 MiB of HBM per device.

v0:
```python
import jax
import jax.numpy as jnp
from jax import lax
from jax.sharding import PartitionSpec as P

ROUNDS = 2
SWEEPS = 2


def softmax_groups(logits):
    largest = jnp.max(logits, axis=0, keepdims=True)
    weights = jnp.exp(logits - largest)
    return weights / jnp.sum(weights, axis=0, keepdims=True)


def group_product(affinity, messages):
    return jnp.dot(
        affinity, messages, precision=lax.Precision.HIGHEST, preferred_element_type=jnp.float32
    )


def node_sums(cavity, membership):
    return jnp.dot(
        cavity, membership, precision=lax.Precision.HIGHEST, preferred_element_type=jnp.float32
    )


def deliver(row_block, peer_count):
    shaped = row_block.reshape(row_block.shape[0], peer_count, -1)
    arrived = lax.all_to_all(shaped, "node", split_axis=1, concat_axis=1, tiled=True)
    return arrived.reshape(row_block.shape[0], -1)


def advance(
    cavity, totals, node_base, affinity, in_use, clipped, send_slots, source_slot, peer_count
):
    slot_logit = (node_base + totals)[:, clipped]
    messages = softmax_groups(slot_logit - cavity)
    arrived = deliver(messages[:, send_slots], peer_count)
    candidates = jnp.concatenate([messages, arrived], axis=1)
    renewed = jnp.where(in_use[None, :], candidates[:, source_slot], 0.0)
    product = group_product(affinity, renewed)
    return jnp.log(jnp.where(in_use[None, :], product, 1.0))


def on_device(node_field, first_messages, affinity, group_share, dst_node, send_slots, source_slot):
    node_count = node_field.shape[1]
    peer_count = lax.axis_size("node")
    every_node = node_count * peer_count
    in_use = dst_node < node_count
    clipped = jnp.minimum(dst_node, node_count - 1)
    membership = (dst_node[:, None] == jnp.arange(node_count, dtype=jnp.int32)[None, :]).astype(
        jnp.float32
    )
    base_field = jnp.log(group_share)[:, None] + node_field
    product = group_product(affinity, first_messages)
    cavity = jnp.log(jnp.where(in_use[None, :], product, 1.0))
    totals = node_sums(cavity, membership)
    node_base = base_field
    for round_index in range(ROUNDS):
        belief = softmax_groups(base_field + totals)
        group_mass = lax.psum(jnp.sum(belief, axis=1), "node")
        field_shift = (
            jnp.dot(
                affinity,
                group_mass,
                precision=lax.Precision.HIGHEST,
                preferred_element_type=jnp.float32,
            )
            / every_node
        )
        node_base = base_field - field_shift[:, None]
        for sweep_index in range(SWEEPS):
            cavity = advance(
                cavity,
                totals,
                node_base,
                affinity,
                in_use,
                clipped,
                send_slots,
                source_slot,
                peer_count,
            )
            totals = node_sums(cavity, membership)
    marginals = softmax_groups(node_base + totals)
    return (marginals, cavity)


def solution(mesh):
    placed = (
        P(None, ("parts", "node")),
        P(None, ("parts", "node")),
        P(),
        P(),
        P(("parts", "node")),
        P(("parts", "node")),
        P(("parts", "node")),
    )
    return jax.shard_map(
        on_device,
        mesh=mesh,
        in_specs=placed,
        out_specs=(P(None, ("parts", "node")), P(None, ("parts", "node"))),
        check_vma=False,
    )
```

profile of v0, /device:TPU:0, one launch (start us, length us, event | category | flops | bytes accessed | tf_op | source)
XLA Modules:
  0.0 205.9 jit_solution(15453720765331189085)
XLA Ops:
  0.7 0.8 broadcast_compare_fusion
  1.4 0.7 fusion.41
  3.5 1.3 fusion.4
  4.8 1.7 fusion.55
  6.7 34.9 %psum.14 = f32[64]{0:T(128)S(1)} all-reduce(f32[64]{0:T(128)S(1)} %divide_reduce_fusion.1), channel_id=1, replica_groups=mesh['parts'=2,'node'=16] {'node'}, use_global_device_ids=true, to_apply=%region_3.4 | all-reduce | flops 64 | bytes 512 | tf_op jit(solution)/shard_map/psum | solution.py:62
  42.0 5.5 %gather_fusion = f32[2048,64]{1,0:T(8,128)S(1)} fusion(f32[64,256]{0,1:T(8,128)S(1)} %copy.33, s32[2048]{0:T(1024)S(1)} %fusion.41), kind=kCustom, calls=%fused_computation | custom fusion | bytes 1056768 | tf_op jit(solution)/shard_map/gather | solution.py:37
  48.5 2.8 %gather_fusion.1 = f32[1024,64]{1,0:T(8,128)S(1)} fusion(f32[64,2048]{0,1:T(8,128)S(1)} %copy.35, s32[1024]{0:T(1024)S(1)} %fusion.43), kind=kCustom, calls=%fused_computation.1 | custom fusion | bytes 528384 | tf_op jit(solution)/shard_map/gather | solution.py:39
  51.5 1.0 reshape.167
  52.5 3.5 %all-to-all-start = ((f32[16,1,4096]{2,1,0:T(1,128)}), f32[16,1,4096]{2,1,0:T(1,128)S(1)}, u32[]{:S(2)}, u32[]{:S(2)}) async-start(f32[16,1,4096]{2,1,0:T(1,128)} %reshape.167), calls=%async_computation | async-start | bytes 524288 | tf_op jit(solution)/shard_map/all_to_all | solution.py:30
  56.1 10.0 %all-to-all-done = f32[16,1,4096]{2,1,0:T(1,128)S(1)} async-done(((f32[16,1,4096]{2,1,0:T(1,128)}), f32[16,1,4096]{2,1,0:T(1,128)S(1)}, u32[]{:S(2)}, u32[]{:S(2)}) %all-to-all-start) | async-done | bytes 262176 | tf_op jit(solution)/shard_map/all_to_all | solution.py:30
  66.6 1.3 reduce.6
  69.1 5.5 %gather_fusion.2 = f32[2048,64]{1,0:T(8,128)S(1)} fusion(f32[64,3072]{0,1:T(8,128)S(1)} %copy.38, s32[2048]{0:T(1024)S(1)} %fusion.42), kind=kCustom, calls=%fused_computation.2 | custom fusion | bytes 1056768 | tf_op jit(solution)/shard_map/gather | solution.py:41
  75.6 0.9 fusion.10
  76.5 5.5 %gather_fusion.3 = f32[2048,64]{1,0:T(8,128)S(1)} fusion(f32[64,256]{0,1:T(8,128)S(1)} %copy.40, s32[2048]{0:T(1024)S(1)} %fusion.41), kind=kCustom, calls=%fused_computation.3 | custom fusion | bytes 1056768 | tf_op jit(solution)/shard_map/gather | solution.py:37
  82.9 2.8 %gather_fusion.4 = f32[1024,64]{1,0:T(8,128)S(1)} fusion(f32[64,2048]{0,1:T(8,128)S(1)} %copy.42, s32[1024]{0:T(1024)S(1)} %fusion.43), kind=kCustom, calls=%fused_computation.4 | custom fusion | bytes 528384 | tf_op jit(solution)/shard_map/gather | solution.py:39
  86.3 12.8 %all_to_all.20 = f32[16,1,4096]{2,1,0:T(1,128)S(1)} all-to-all(f32[16,1,4096]{2,1,0:T(1,128)S(1)} %reshape.169), channel_id=1, replica_groups=mesh['parts'=2,'node'=16] {'node'}, dimensions={0} | all-to-all | bytes 524288 | tf_op jit(solution)/shard_map/all_to_all | solution.py:30
  99.1 1.3 reduce.7
  101.6 5.5 %gather_fusion.5 = f32[2048,64]{1,0:T(8,128)S(1)} fusion(f32[64,3072]{0,1:T(8,128)S(1)} %copy.45, s32[2048]{0:T(1024)S(1)} %fusion.42), kind=kCustom, calls=%fused_computation.5 | custom fusion | bytes 1056768 | tf_op jit(solution)/shard_map/gather | solution.py:41
  108.1 0.9 fusion.53
  109.2 30.9 %psum.15 = f32[64]{0:T(128)S(1)} all-reduce(f32[64]{0:T(128)S(1)} %divide_reduce_fusion), channel_id=1, replica_groups=mesh['parts'=2,'node'=16] {'node'}, use_global_device_ids=true, to_apply=%region_11.12 | all-reduce | flops 64 | bytes 512 | tf_op jit(solution)/shard_map/psum | solution.py:62
  140.4 5.5 %gather_fusion.6 = f32[2048,64]{1,0:T(8,128)S(1)} fusion(f32[64,256]{0,1:T(8,128)S(1)} %copy.47, s32[2048]{0:T(1024)S(1)} %fusion.41), kind=kCustom, calls=%fused_computation.6 | custom fusion | bytes 1056768 | tf_op jit(solution)/shard_map/gather | solution.py:37
  146.8 2.8 %gather_fusion.7 = f32[1024,64]{1,0:T(8,128)S(1)} fusion(f32[64,2048]{0,1:T(8,128)S(1)} %copy.49, s32[1024]{0:T(1024)S(1)} %fusion.43), kind=kCustom, calls=%fused_computation.7 | custom fusion | bytes 528384 | tf_op jit(solution)/shard_map/gather | solution.py:39
  150.1 12.6 %all_to_all.21 = f32[16,1,4096]{2,1,0:T(1,128)S(1)} all-to-all(f32[16,1,4096]{2,1,0:T(1,128)S(1)} %reshape.171), channel_id=1, replica_groups=mesh['parts'=2,'node'=16] {'node'}, dimensions={0} | all-to-all | bytes 524288 | tf_op jit(solution)/shard_map/all_to_all | solution.py:30
  162.8 1.3 reduce.8
  165.3 5.5 %gather_fusion.8 = f32[2048,64]{1,0:T(8,128)S(1)} fusion(f32[64,3072]{0,1:T(8,128)S(1)} %copy.52, s32[2048]{0:T(1024)S(1)} %fusion.42), kind=kCustom, calls=%fused_computation.8 | custom fusion | bytes 1056768 | tf_op jit(solution)/shard_map/gather | solution.py:41
  171.7 0.9 fusion.11
  172.7 5.5 %gather_fusion.9 = f32[2048,64]{1,0:T(8,128)S(1)} fusion(f32[64,256]{0,1:T(8,128)S(1)} %copy.54, s32[2048]{0:T(1024)S(1)} %fusion.41), kind=kCustom, calls=%fused_computation.9 | custom fusion | bytes 1056768 | tf_op jit(solution)/shard_map/gather | solution.py:37
  179.1 2.8 %gather_fusion.10 = f32[1024,64]{1,0:T(8,128)S(1)} fusion(f32[64,2048]{0,1:T(8,128)S(1)} %copy.56, s32[1024]{0:T(1024)S(1)} %fusion.43), kind=kCustom, calls=%fused_computation.10 | custom fusion | bytes 528384 | tf_op jit(solution)/shard_map/gather | solution.py:39
  182.5 12.8 %all_to_all.22 = f32[16,1,4096]{2,1,0:T(1,128)S(1)} all-to-all(f32[16,1,4096]{2,1,0:T(1,128)S(1)} %reshape.173), channel_id=1, replica_groups=mesh['parts'=2,'node'=16] {'node'}, dimensions={0} | all-to-all | bytes 524288 | tf_op jit(solution)/shard_map/all_to_all | solution.py:30
  195.3 1.3 reduce.9
  197.8 5.5 %gather_fusion.11 = f32[2048,64]{1,0:T(8,128)S(1)} fusion(f32[64,3072]{0,1:T(8,128)S(1)} %copy.59, s32[2048]{0:T(1024)S(1)} %fusion.42), kind=kCustom, calls=%fused_computation.11 | custom fusion | bytes 1056768 | tf_op jit(solution)/shard_map/gather | solution.py:41
  204.3 0.9 fusion.56
  (85 shorter events, 17.9 us)
Async XLA Ops:
  0.6 2.9 %copy-start = (f32[64,2048]{1,0:T(8,128)S(1)}, f32[64,2048]{1,0:T(8,128)}, u32[]{:S(2)}) copy-start(f32[64,2048]{1,0:T(8,128)} %param.8) | copy-start | bytes 1572868
  0.6 41.0 %copy-start.1 = (f32[64,64]{1,0:T(8,128)S(1)}, f32[64,64]{1,0:T(8,128)}, u32[]{:S(2)}) copy-start(f32[64,64]{1,0:T(8,128)} %param.9) | copy-start | bytes 49156
  0.7 41.2 %copy-start.3 = (f32[64,256]{1,0:T(8,128)S(1)}, f32[64,256]{1,0:T(8,128)}, u32[]{:S(2)}) copy-start(f32[64,256]{1,0:T(8,128)} %param.7) | copy-start | bytes 196612
  51.3 4.8 %copy-start.5 = (s32[2048]{0:T(1024)S(1)}, s32[2048]{0:T(1024)}, u32[]{:S(2)}) copy-start(s32[2048]{0:T(1024)} %param.13) | copy-start | bytes 24580
  52.5 13.5 %all-to-all-start = ((f32[16,1,4096]{2,1,0:T(1,128)}), f32[16,1,4096]{2,1,0:T(1,128)S(1)}, u32[]{:S(2)}, u32[]{:S(2)}) async-start(f32[16,1,4096]{2,1,0:T(1,128)} %reshape.167), calls=%async_computation | async-start | bytes 524288 | tf_op jit(solution)/shard_map/all_to_all | solution.py:30
  74.6 1.0 copy-start.4
  204.3 1.6 copy-start.2
where the time goes:
time: 206 us
  blocking collectives  104 us (50%)
  local copies, waits for them, and re-layouts  67.8 us (33%)
  waiting for transfers between devices  9.98 us (5%)
  other arithmetic  9.68 us (5%)
  matrix products  9.52 us (5%)
  starting transfers between devices  3.53 us (2%)
    psum x2, blocking collectives, on_device(): group_mass = lax.psum(jnp.sum(belief, axis=1), 'node')  65.8 us
    all_to_all x3, blocking collectives, deliver(): lax.all_to_all(shaped, 'node', split_axis=1, concat_axis=1, tiled=True)  38.3 us
    gather x8, local copies, waits for them, and re-layouts, advance(): slot_logit = (node_base + totals)[:, clipped]  23.1 us
    gather x8, local copies, waits for them, and re-layouts, advance(): renewed = jnp.where(in_use[None, :], candidates[:, source_slot], 0.0)  23.1 us
    gather x4, local copies, waits for them, and re-layouts, advance(): arrived = deliver(messages[:, send_slots], peer_count)  11.3 us
    all_to_all x1, waiting for transfers between devices, deliver(): lax.all_to_all(shaped, 'node', split_axis=1, concat_axis=1, tiled=True)  9.98 us
    dot_general x5, matrix products, node_sums(): jnp.dot(cavity, membership, precision=lax.Precision.HIGHEST, preferred_el...  5.25 us
    all_to_all x4, other arithmetic, deliver(): lax.all_to_all(shaped, 'node', split_axis=1, concat_axis=1, tiled=True)  5.04 us
  transfers between devices with their start and end apart: 1, of which 1 were waited for; matrix products, arithmetic and copies ran while one was open for 0% of the time, Pallas kernels for 0%

commit v1 on v0

v1 whole, which is shorter than its diff:
```python
import functools

import jax
import jax.numpy as jnp
from jax import lax
from jax.experimental import pallas as pl
from jax.experimental.pallas import tpu as pltpu
from jax.sharding import PartitionSpec as P

ROUNDS = 2
SWEEPS = 2
TILE = 256
F32 = jnp.float32
BF16 = jnp.bfloat16
LAST = (((1,), (1,)), ((), ()))


def split_three(x):
    high = x.astype(BF16)
    rest = x - high.astype(F32)
    middle = rest.astype(BF16)
    low = (rest - middle.astype(F32)).astype(BF16)
    return jnp.concatenate([high, middle, low], axis=0)


def join_three(x):
    g = x.shape[0] // 3
    return x[:g] + x[g : 2 * g] + x[2 * g :]


def softmax_groups(logits):
    weights = jnp.exp(logits - jnp.max(logits, axis=0, keepdims=True))
    return weights / jnp.sum(weights, axis=0, keepdims=True)


def loop(count, body, init):
    return lax.fori_loop(0, count, body, init, unroll=count <= 4)


def kernel(
    n, field_ref, first_ref, aff_ref, share_ref, dst_ref, send_ref, own_ref, src_ref,
    marg_ref, out_ref,
    vals, cav, member, live, chosen, pos_ref, partner, sbuf, rbuf, mass_out, mass_in,
    send_sem, recv_sem, msend_sem, mrecv_sem,
):
    me = lax.axis_index("node")
    groups, nodes = field_ref.shape
    slots = first_ref.shape[1]
    places = send_ref.shape[1]
    cap = places // n
    pairs = slots // 2
    width = 512
    every_node = nodes * n

    barrier = pltpu.get_barrier_semaphore()

    @pl.loop(1, n)
    def _(i):
        pl.semaphore_signal(
            barrier, inc=1, device_id={"node": lax.rem(me + i, n)},
            device_id_type=pl.DeviceIdType.MESH,
        )

    aff = aff_ref[...]
    aff_high = aff.astype(BF16)
    aff_mid = (aff - aff_high.astype(F32)).astype(BF16)
    aff_wide = jnp.concatenate([aff_high, aff_high, aff_mid, aff_mid], axis=1)

    def group_logs(messages, alive):
        high = messages.astype(BF16)
        mid = (messages - high.astype(F32)).astype(BF16)
        stacked = jnp.concatenate([high, mid, high, mid], axis=0)
        product = jnp.dot(aff_wide, stacked, preferred_element_type=F32)
        return jnp.log(jnp.where(alive, product, 1.0))

    dst = dst_ref[...]
    src = src_ref[...]
    in_use = dst < nodes
    own = own_ref[pl.ds(me, 1), :]
    row16 = lax.broadcasted_iota(jnp.int32, (16, cap), 0)
    own_digits = jnp.where(row16 == 0, own >> 6, own & 63).astype(F32).astype(BF16)
    own_hot = jnp.where(
        lax.broadcasted_iota(jnp.int32, (cap, slots), 0) == src - (slots + me * cap), 1.0, 0.0
    ).astype(BF16)
    own_slot = jnp.dot(own_digits, own_hot, preferred_element_type=F32)
    own_slot = (own_slot[0:1] * 64.0 + own_slot[1:2]).astype(jnp.int32)
    through_own = (src >= slots + me * cap) & (src < slots + (me + 1) * cap)
    src = jnp.where(through_own, own_slot, src)
    slot_id = lax.broadcasted_iota(jnp.int32, (1, slots), 1)
    leads = in_use & (src < slots) & (src > slot_id)
    lead_f = jnp.where(leads, 1.0, 0.0)
    before = jnp.where(
        lax.broadcasted_iota(jnp.int32, (TILE, TILE), 0)
        < lax.broadcasted_iota(jnp.int32, (TILE, TILE), 1), 1.0, 0.0,
    ).astype(BF16)
    carry = jnp.zeros((1, 1), F32)
    ranks = []
    for c in range(slots // TILE):
        piece = lead_f[:, c * TILE : (c + 1) * TILE]
        inner = jnp.dot(
            jnp.broadcast_to(piece, (16, TILE)).astype(BF16), before, preferred_element_type=F32
        )[0:1]
        ranks.append(inner + carry)
        carry = carry + jnp.sum(piece, axis=1, keepdims=True)
    rank = jnp.concatenate(ranks, axis=1).astype(jnp.int32)
    position = jnp.where(
        leads, places + rank, jnp.where(in_use & (src >= slots), src - slots, -1)
    )
    pos_ref[...] = jnp.broadcast_to(position, pos_ref.shape)

    row = lax.broadcasted_iota(jnp.int32, (16, slots), 0)
    src1 = src + 1
    slot1 = slot_id + 1
    digits = jnp.where(
        row == 0, dst + 1,
        jnp.where(
            row == 1, src1 >> 6,
            jnp.where(row == 2, src1 & 63, jnp.where(row == 3, slot1 >> 6, slot1 & 63)),
        ),
    )
    vals[3 * groups :, :] = digits.astype(F32).astype(BF16)

    def start_logs(c, _):
        cols = pl.ds(pl.multiple_of(c * width, width), width)
        vals[: 3 * groups, cols] = split_three(
            group_logs(first_ref[:, cols], dst_ref[:, cols] < nodes)
        )
        return 0

    loop(slots // width, start_logs, 0)

    node_id = lax.broadcasted_iota(jnp.int32, (nodes, TILE), 0)

    def keep(cols, moved):
        cav[:, cols] = join_three(moved[: 3 * groups])
        node1 = moved[3 * groups : 3 * groups + 1].astype(jnp.int32)
        member[:, cols] = jnp.where(node_id + 1 == node1, 1.0, 0.0).astype(BF16)
        live[:, cols] = jnp.broadcast_to(node1, (8, TILE))

    def to_slot(start):
        ids = lax.broadcasted_iota(jnp.int32, (TILE, slots), 0) + start
        return jnp.where(ids == pos_ref[0:1, :], 1.0, 0.0).astype(BF16)

    def from_partner(c):
        cols = pl.ds(pl.multiple_of(c * TILE, TILE), TILE)
        ids = lax.broadcasted_iota(jnp.int32, (slots, TILE), 0)
        return jnp.where(ids == partner[0:1, cols], 1.0, 0.0).astype(BF16)

    def place_received(c, _):
        start = pl.multiple_of(c * TILE, TILE)
        hot = to_slot(start)
        keep(pl.ds(start, TILE), lax.dot_general(vals[...], hot, LAST, preferred_element_type=F32))
        held = lax.dot_general(hot, vals[3 * groups :, :], LAST, preferred_element_type=F32)
        held = (held[:, 3:4] * 64.0 + held[:, 4:5]).astype(jnp.int32) - 1
        chosen[c] = jnp.where(held == send_ref[:, pl.ds(start, TILE)], 1.0, 0.0).astype(BF16)
        return 0

    lax.fori_loop(0, places // TILE, place_received, 0)

    def place_pairs(c, _):
        start = pl.multiple_of(places + c * TILE, TILE)
        moved = lax.dot_general(vals[...], to_slot(start), LAST, preferred_element_type=F32)
        keep(pl.ds(start, TILE), moved)
        other = moved[3 * groups + 1 : 3 * groups + 2] * 64.0 + moved[3 * groups + 2 : 3 * groups + 3]
        cols = pl.ds(pl.multiple_of(c * TILE, TILE), TILE)
        partner[:, cols] = jnp.broadcast_to(other.astype(jnp.int32) - 1, (8, TILE))
        moved = jnp.dot(vals[...], from_partner(c), preferred_element_type=F32)
        keep(pl.ds(pl.multiple_of(start + pairs, TILE), TILE), moved)
        return 0

    lax.fori_loop(0, pairs // TILE, place_pairs, 0)

    for step in range(ROUNDS * SWEEPS):
        rbuf[step, me] = jnp.zeros(rbuf.shape[2:], F32)

    def add_up(acc, cols, terms):
        return acc + lax.dot_general(
            split_three(terms), member[:, cols], LAST, preferred_element_type=F32
        )

    def sum_start(c, acc):
        cols = pl.ds(pl.multiple_of(c * width, width), width)
        return add_up(acc, cols, cav[:, cols])

    zero = jnp.zeros((3 * groups, nodes), F32)
    totals = join_three(loop((places + slots) // width, sum_start, zero))
    base = jnp.log(share_ref[...]) + field_ref[...]
    half = lax.broadcasted_iota(jnp.int32, (groups // 2, 2 * cap), 1) < cap
    pl.semaphore_wait(barrier, n - 1)

    node_base = base
    weight = jnp.ones((groups, 1), F32)
    for round_index in range(ROUNDS):
        for sweep_index in range(SWEEPS):
            step = round_index * SWEEPS + sweep_index
            late = sweep_index == 0
            if late:
                belief = softmax_groups(base + totals)
                mass = lax.dot_general(
                    jnp.ones((8, nodes), BF16), split_three(belief), LAST,
                    preferred_element_type=F32,
                )
                mass = mass[:, :groups] + mass[:, groups : 2 * groups] + mass[:, 2 * groups :]
                mass = jnp.concatenate([mass, jnp.zeros_like(mass)], axis=1)
                mass_out[round_index] = mass
                mass_in[round_index, me] = mass

                @pl.loop(1, n)
                def _(i):
                    pltpu.make_async_remote_copy(
                        src_ref=mass_out.at[round_index], dst_ref=mass_in.at[round_index, me],
                        send_sem=msend_sem.at[round_index], recv_sem=mrecv_sem.at[round_index],
                        device_id={"node": lax.rem(me + i, n)},
                        device_id_type=pl.DeviceIdType.MESH,
                    ).start()

            logit = (base if late else node_base) + totals
            logit = split_three(logit - jnp.max(logit, axis=0, keepdims=True))

            def outgoing(cols):
                at_slot = join_three(jnp.dot(logit, member[:, cols], preferred_element_type=F32))
                at_slot = at_slot - cav[:, cols]
                return jnp.exp(at_slot - jnp.max(at_slot, axis=0, keepdims=True))

            def send_part(c, _):
                start = pl.multiple_of(c * TILE, TILE)
                out = outgoing(pl.ds(start, TILE))
                out = join_three(
                    jnp.dot(split_three(out), chosen[c], preferred_element_type=F32)
                )
                for j in range(TILE // (2 * cap)):
                    x = out[:, j * 2 * cap : (j + 1) * 2 * cap]
                    r = pltpu.roll(x, cap, 1)
                    peer = c * (TILE // cap) + 2 * j
                    sbuf[step, peer] = jnp.where(half, x[: groups // 2], r[groups // 2 :])
                    sbuf[step, peer + 1] = jnp.where(half, r[: groups // 2], x[groups // 2 :])
                return 0

            loop(places // TILE, send_part, 0)

            @pl.loop(1, n)
            def _(i):
                peer = lax.rem(me + i, n)
                pltpu.make_async_remote_copy(
                    src_ref=sbuf.at[step, peer], dst_ref=rbuf.at[step, me],
                    send_sem=send_sem.at[step], recv_sem=recv_sem.at[step],
                    device_id={"node": peer}, device_id_type=pl.DeviceIdType.MESH,
                ).start()

            if late:
                arrived = mass_in.at[round_index, pl.ds(0, n - 1)]
                pltpu.make_async_copy(arrived, arrived, mrecv_sem.at[round_index]).wait()
                mass = loop(
                    n, lambda b, acc: acc + mass_in[round_index, b], jnp.zeros((8, 2 * cap), F32)
                )
                shift = jnp.sum(aff * mass[0:1, :groups], axis=1, keepdims=True) / every_node
                node_base = base - shift
                weight = jnp.exp(jnp.min(shift, axis=0, keepdims=True) - shift)

            def renew(cols, messages):
                messages = messages * weight
                scale = jnp.maximum(jnp.sum(messages, axis=0, keepdims=True), 1e-30)
                return group_logs(messages / scale, live[0:1, cols] > 0)

            if not late:
                weight = jnp.ones((groups, 1), F32)

            def local_part(c, acc):
                lead = pl.ds(pl.multiple_of(places + c * width, width), width)
                back = pl.ds(pl.multiple_of(places + pairs + c * width, width), width)
                lead_out, back_out = outgoing(lead), outgoing(back)
                lead_new, back_new = renew(lead, back_out), renew(back, lead_out)
                cav[:, lead] = lead_new
                cav[:, back] = back_new
                return add_up(add_up(acc, lead, lead_new), back, back_new)

            acc = loop(pairs // width, local_part, zero)

            arrived = rbuf.at[step, pl.ds(0, n - 1)]
            pltpu.make_async_copy(arrived, arrived, recv_sem.at[step]).wait()

            def take_part(c, acc):
                cols = pl.ds(pl.multiple_of(c * width, width), width)
                tiles = []
                for j in range(width // (2 * cap)):
                    peer = c * (width // cap) + 2 * j
                    b0, b1 = rbuf[step, peer], rbuf[step, peer + 1]
                    top = jnp.where(half, b0, pltpu.roll(b1, cap, 1))
                    low = jnp.where(half, pltpu.roll(b0, cap, 1), b1)
                    tiles.append(jnp.concatenate([top, low], axis=0))
                fresh = renew(cols, jnp.concatenate(tiles, axis=1))
                cav[:, cols] = fresh
                return add_up(acc, cols, fresh)

            totals = join_three(loop(places // width, take_part, acc))

    marg_ref[...] = softmax_groups(node_base + totals)

    out_ref[...] = jnp.zeros_like(out_ref)

    def back_first(c, _):
        start = pl.multiple_of(c * TILE, TILE)
        terms = split_three(cav[:, pl.ds(start, TILE)])
        out_ref[...] += join_three(jnp.dot(terms, to_slot(start), preferred_element_type=F32))
        return 0

    lax.fori_loop(0, (places + pairs) // TILE, back_first, 0)

    def back_partner(c, _):
        start = pl.multiple_of(places + pairs + c * TILE, TILE)
        terms = split_three(cav[:, pl.ds(start, TILE)])
        out_ref[...] += join_three(
            lax.dot_general(terms, from_partner(c), LAST, preferred_element_type=F32)
        )
        return 0

    lax.fori_loop(0, pairs // TILE, back_partner, 0)

    for step in range(ROUNDS * SWEEPS):
        sent = sbuf.at[step, pl.ds(0, n - 1)]
        pltpu.make_async_copy(sent, sent, send_sem.at[step]).wait()
    for round_index in range(ROUNDS):
        sent = mass_in.at[round_index, pl.ds(0, n - 1)]
        pltpu.make_async_copy(sent, sent, msend_sem.at[round_index]).wait()


def on_device(node_field, first_messages, affinity, group_share, dst_node, send_slots, source_slot):
    n = lax.axis_size("node")
    groups, nodes = node_field.shape
    slots = first_messages.shape[1]
    places = send_slots.shape[0]
    cap = places // n
    steps = ROUNDS * SWEEPS
    total = places + slots
    vmem = pl.BlockSpec(memory_space=pltpu.VMEM)
    return pl.pallas_call(
        functools.partial(kernel, n),
        out_shape=(
            jax.ShapeDtypeStruct((groups, nodes), F32),
            jax.ShapeDtypeStruct((groups, slots), F32),
        ),
        in_specs=[vmem] * 8,
        out_specs=(vmem, vmem),
        scratch_shapes=[
            pltpu.VMEM((3 * groups + 16, slots), BF16),
            pltpu.VMEM((groups, total), F32),
            pltpu.VMEM((nodes, total), BF16),
            pltpu.VMEM((8, total), jnp.int32),
            pltpu.VMEM((places // TILE, TILE, TILE), BF16),
            pltpu.VMEM((8, slots), jnp.int32),
            pltpu.VMEM((8, slots // 2), jnp.int32),
            pltpu.VMEM((steps, n, groups // 2, 2 * cap), F32),
            pltpu.VMEM((steps, n, groups // 2, 2 * cap), F32),
            pltpu.VMEM((ROUNDS, 8, 2 * cap), F32),
            pltpu.VMEM((ROUNDS, n, 8, 2 * cap), F32),
            pltpu.SemaphoreType.DMA((steps,)),
            pltpu.SemaphoreType.DMA((steps,)),
            pltpu.SemaphoreType.DMA((ROUNDS,)),
            pltpu.SemaphoreType.DMA((ROUNDS,)),
        ],
        compiler_params=pltpu.CompilerParams(
            collective_id=0, has_side_effects=True, vmem_limit_bytes=52 * 1024 * 1024
        ),
    )(
        node_field,
        first_messages,
        affinity,
        group_share.reshape(groups, 1),
        dst_node.reshape(1, slots),
        send_slots.reshape(1, places),
        send_slots.reshape(n, cap),
        source_slot.reshape(1, slots),
    )


def solution(mesh):
    split = P(None, ("parts", "node"))
    flat = P(("parts", "node"))
    return jax.shard_map(
        on_device,
        mesh=mesh,
        in_specs=(split, split, P(), P(), flat, flat, flat),
        out_specs=(split, split),
        check_vma=False,
    )
```

time: 206 us -> 61.3 us (0.30)
  blocking collectives: 104 us -> 0 us
  local copies, waits for them, and re-layouts: 67.8 us -> 4.82 us
  Pallas kernels: 0 us -> 55.4 us
  waiting for transfers between devices: 9.98 us -> 0 us
  other arithmetic: 9.68 us -> 0 us
  matrix products: 9.52 us -> 0 us
  starting transfers between devices: 3.53 us -> 0 us
    psum x2 -> x0, blocking collectives: 65.8 us -> none  [on_device(): group_mass = lax.psum(jnp.sum(belief, axis=1), 'node')]
    gather x20 -> x0, local copies, waits for them, and re-layouts: 57.5 us -> none  [the longest x8 23.1 us: advance(): slot_logit = (node_base + totals)[:, clipped]]
    pallas_call x0 -> x1, Pallas kernels: none -> 55.4 us  [on_device(): pl.pallas_call(functools.partial(kernel, n), out_shape=(jax.ShapeDtypeStr...]
    all_to_all x3 -> x0, blocking collectives: 38.3 us -> none  [deliver(): lax.all_to_all(shaped, 'node', split_axis=1, concat_axis=1, tiled=True)]
    all_to_all x1 -> x0, waiting for transfers between devices: 9.98 us -> none  [deliver(): lax.all_to_all(shaped, 'node', split_axis=1, concat_axis=1, tiled=True)]
    dot_general x12 -> x0, matrix products: 9.52 us -> none  [the longest x5 5.25 us: node_sums(): jnp.dot(cavity, membership, precision=lax.Precision.HIGHEST, preferred_el...]
    all_to_all x4 -> x0, other arithmetic: 5.04 us -> none  [deliver(): lax.all_to_all(shaped, 'node', split_axis=1, concat_axis=1, tiled=True)]
    all_to_all x1 -> x0, starting transfers between devices: 3.53 us -> none  [deliver(): lax.all_to_all(shaped, 'node', split_axis=1, concat_axis=1, tiled=True)]
  transfers between devices with their start and end apart: 1 -> 0, of which waited for: 1 -> 0; matrix products, arithmetic and copies ran while one was open for 0% -> 0% of each run, Pallas kernels for 0% -> 0%
where the time goes in v1:
time: 61.3 us; the launch traced here: 60.9 us
  Pallas kernels  55.4 us (90%)
  local copies, waits for them, and re-layouts  4.82 us (8%)
  between operations  0.68 us (1%)
    pallas_call x1, Pallas kernels, on_device(): pl.pallas_call(functools.partial(kernel, n), out_shape=(jax.ShapeDtypeStr...  55.4 us
    unnamed x14, local copies, waits for them, and re-layouts  3.98 us

profile of v1, /device:TPU:0, one launch (start us, length us, event | category | flops | bytes accessed | tf_op | source)
XLA Modules:
  0.0 60.9 jit_solution(2155669570766318610)
XLA Ops:
  0.6 0.0 copy-start.3
  0.6 0.0 copy-start.2
  0.6 0.7 %copy-done.3 = s32[1024]{0:T(1024)S(1)} copy-done((s32[1024]{0:T(1024)S(1)}, s32[1024]{0:T(1024)}, u32[]{:S(2)}) %copy-start.3) | copy-done | bytes 4120
  1.3 0.1 reshape.22.own_ref
  1.4 0.0 copy-start.4
  1.4 0.0 copy-start.5
  1.4 0.8 %copy.9.share_ref = f32[64,1]{1,0:T(8,128)S(1)} copy(f32[64,1]{0,1:T(1,128)} %bitcast.7) | data formatting | bytes 512 | tf_op jit(solution)/shard_map/reshape | solution.py:368
  2.2 0.0 copy-done.2
  2.2 0.0 copy-done.4
  2.2 0.0 copy-done.5
  2.2 0.0 copy-start
  2.2 1.0 %copy-done = f32[64,2048]{1,0:T(8,128)S(1)} copy-done((f32[64,2048]{1,0:T(8,128)S(1)}, f32[64,2048]{1,0:T(8,128)}, u32[]{:S(2)}) %copy-start) | copy-done | bytes 524312
  3.2 0.0 copy-start.1
  3.2 0.8 %copy-done.1 = f32[64,256]{1,0:T(8,128)S(1)} copy-done((f32[64,256]{1,0:T(8,128)S(1)}, f32[64,256]{1,0:T(8,128)}, u32[]{:S(2)}) %copy-start.1) | copy-done | bytes 65560
  4.1 55.4 %shard_map.86 = (f32[64,256]{1,0:T(8,128)S(1)}, f32[64,2048]{1,0:T(8,128)S(1)}) custom-call(f32[64,256]{1,0:T(8,128)S(1)} %copy-done.1, f32[64,2048]{1,0:T(8,128)S(1)} %copy-done, f32[64,64]{1,0:T(8,128)S(1)} %copy-done.2, f32[64,1]{1,0:T(8,128)S(1)} %copy.9.share_ref, s32[1,2048]{1,0:T(1,128)S(1)} %bitcast.5, s32[1,1024]{1,0:T(1,128)S(1)} %bitcast.4, ...), custom_call_target="tpu_custom_call" | custom-call | tf_op jit(solution)/shard_map/pallas_call | solution.py:336
  59.5 0.6 %copy.12 = f32[64,256]{1,0:T(8,128)} copy(f32[64,256]{1,0:T(8,128)S(1)} %get-tuple-element.4) | data formatting | bytes 131072
  60.1 0.8 %copy.13 = f32[64,2048]{1,0:T(8,128)} copy(f32[64,2048]{1,0:T(8,128)S(1)} %get-tuple-element.5) | data formatting | bytes 1048576
Async XLA Ops:
  0.6 0.7 %copy-start.3 = (s32[1024]{0:T(1024)S(1)}, s32[1024]{0:T(1024)}, u32[]{:S(2)}) copy-start(s32[1024]{0:T(1024)} %param.12) | copy-start | bytes 12292
  0.6 1.5 %copy-start.2 = (f32[64,64]{1,0:T(8,128)S(1)}, f32[64,64]{1,0:T(8,128)}, u32[]{:S(2)}) copy-start(f32[64,64]{1,0:T(8,128)} %aff_ref.1) | copy-start | bytes 49156
  1.4 0.8 %copy-start.4 = (s32[2048]{0:T(1024)S(1)}, s32[2048]{0:T(1024)}, u32[]{:S(2)}) copy-start(s32[2048]{0:T(1024)} %param.11) | copy-start | bytes 24580
  1.4 0.8 %copy-start.5 = (s32[2048]{0:T(1024)S(1)}, s32[2048]{0:T(1024)}, u32[]{:S(2)}) copy-start(s32[2048]{0:T(1024)} %param.13) | copy-start | bytes 24580
  2.2 1.0 %copy-start = (f32[64,2048]{1,0:T(8,128)S(1)}, f32[64,2048]{1,0:T(8,128)}, u32[]{:S(2)}) copy-start(f32[64,2048]{1,0:T(8,128)} %first_ref.1) | copy-start | bytes 1572868
  3.2 0.8 %copy-start.1 = (f32[64,256]{1,0:T(8,128)S(1)}, f32[64,256]{1,0:T(8,128)}, u32[]{:S(2)}) copy-start(f32[64,256]{1,0:T(8,128)} %field_ref.1) | copy-start | bytes 196612

commit v2 on v1

--- a/solution.py
+++ b/solution.py
@@ -50,6 +50,10 @@
     cap = places // n
     pairs = slots // 2
     width = 512
+    planes = places // TILE
+    group = TILE // cap
+    plane = me // group
+    far_first = sorted(range(planes), key=lambda o: (-min(o, planes - o), o))
     every_node = nodes * n
 
     barrier = pltpu.get_barrier_semaphore()
@@ -120,14 +124,17 @@
     )
     vals[3 * groups :, :] = digits.astype(F32).astype(BF16)
 
-    def start_logs(c, _):
+    zero = jnp.zeros((3 * groups, nodes), F32)
+
+    def start_logs(c, acc):
         cols = pl.ds(pl.multiple_of(c * width, width), width)
-        vals[: 3 * groups, cols] = split_three(
-            group_logs(first_ref[:, cols], dst_ref[:, cols] < nodes)
-        )
-        return 0
-
-    loop(slots // width, start_logs, 0)
+        terms = split_three(group_logs(first_ref[:, cols], dst_ref[:, cols] < nodes))
+        vals[: 3 * groups, cols] = terms
+        ids = lax.broadcasted_iota(jnp.int32, (nodes, width), 0)
+        hot = jnp.where(ids == dst_ref[:, cols], 1.0, 0.0).astype(BF16)
+        return acc + lax.dot_general(terms, hot, LAST, preferred_element_type=F32)
+
+    totals = join_three(loop(slots // width, start_logs, zero))
 
     node_id = lax.broadcasted_iota(jnp.int32, (nodes, TILE), 0)
 
@@ -168,8 +175,6 @@
         keep(pl.ds(pl.multiple_of(start + pairs, TILE), TILE), moved)
         return 0
 
-    lax.fori_loop(0, pairs // TILE, place_pairs, 0)
-
     for step in range(ROUNDS * SWEEPS):
         rbuf[step, me] = jnp.zeros(rbuf.shape[2:], F32)
 
@@ -178,13 +183,25 @@
             split_three(terms), member[:, cols], LAST, preferred_element_type=F32
         )
 
-    def sum_start(c, acc):
-        cols = pl.ds(pl.multiple_of(c * width, width), width)
-        return add_up(acc, cols, cav[:, cols])
-
-    zero = jnp.zeros((3 * groups, nodes), F32)
-    totals = join_three(loop((places + slots) // width, sum_start, zero))
-    base = jnp.log(share_ref[...]) + field_ref[...]
+    square = (groups, groups)
+    diagonal = lax.broadcasted_iota(jnp.int32, square, 0) == lax.broadcasted_iota(jnp.int32, square, 1)
+    share = jnp.sum(jnp.where(diagonal, share_ref[...], 0.0), axis=1, keepdims=True)
+    base = jnp.log(share) + field_ref[...]
+
+    def back_first(c, _):
+        start = pl.multiple_of(c * TILE, TILE)
+        terms = split_three(cav[:, pl.ds(start, TILE)])
+        out_ref[...] += join_three(jnp.dot(terms, to_slot(start), preferred_element_type=F32))
+        return 0
+
+    def back_partner(c, _):
+        start = pl.multiple_of(places + pairs + c * TILE, TILE)
+        terms = split_three(cav[:, pl.ds(start, TILE)])
+        out_ref[...] += join_three(
+            lax.dot_general(terms, from_partner(c), LAST, preferred_element_type=F32)
+        )
+        return 0
+
     half = lax.broadcasted_iota(jnp.int32, (groups // 2, 2 * cap), 1) < cap
     pl.semaphore_wait(barrier, n - 1)
 
@@ -194,26 +211,6 @@
         for sweep_index in range(SWEEPS):
             step = round_index * SWEEPS + sweep_index
             late = sweep_index == 0
-            if late:
-                belief = softmax_groups(base + totals)
-                mass = lax.dot_general(
-                    jnp.ones((8, nodes), BF16), split_three(belief), LAST,
-                    preferred_element_type=F32,
-                )
-                mass = mass[:, :groups] + mass[:, groups : 2 * groups] + mass[:, 2 * groups :]
-                mass = jnp.concatenate([mass, jnp.zeros_like(mass)], axis=1)
-                mass_out[round_index] = mass
-                mass_in[round_index, me] = mass
-
-                @pl.loop(1, n)
-                def _(i):
-                    pltpu.make_async_remote_copy(
-                        src_ref=mass_out.at[round_index], dst_ref=mass_in.at[round_index, me],
-                        send_sem=msend_sem.at[round_index], recv_sem=mrecv_sem.at[round_index],
-                        device_id={"node": lax.rem(me + i, n)},
-                        device_id_type=pl.DeviceIdType.MESH,
-                    ).start()
-
             logit = (base if late else node_base) + totals
             logit = split_three(logit - jnp.max(logit, axis=0, keepdims=True))
 
@@ -234,24 +231,56 @@
                     peer = c * (TILE // cap) + 2 * j
                     sbuf[step, peer] = jnp.where(half, x[: groups // 2], r[groups // 2 :])
                     sbuf[step, peer + 1] = jnp.where(half, r[: groups // 2], x[groups // 2 :])
+                for j in range(group):
+                    peer = c * group + j
+
+                    @pl.when(peer != me)
+                    def _():
+                        pltpu.make_async_remote_copy(
+                            src_ref=sbuf.at[step, peer], dst_ref=rbuf.at[step, me],
+                            send_sem=send_sem.at[step], recv_sem=recv_sem.at[step, plane],
+                            device_id={"node": peer}, device_id_type=pl.DeviceIdType.MESH,
+                        ).start()
+
                 return 0
 
-            loop(places // TILE, send_part, 0)
-
-            @pl.loop(1, n)
-            def _(i):
-                peer = lax.rem(me + i, n)
-                pltpu.make_async_remote_copy(
-                    src_ref=sbuf.at[step, peer], dst_ref=rbuf.at[step, me],
-                    send_sem=send_sem.at[step], recv_sem=recv_sem.at[step],
-                    device_id={"node": peer}, device_id_type=pl.DeviceIdType.MESH,
-                ).start()
+            if planes <= 4:
+                for k in far_first:
+                    send_part(lax.rem(plane + k, planes), 0)
+            else:
+                lax.fori_loop(
+                    0, planes,
+                    lambda k, x: send_part(lax.rem(plane + planes // 2 + k, planes), x), 0,
+                )
+
+            if late:
+                belief = softmax_groups(base + totals)
+                mass = lax.dot_general(
+                    jnp.ones((8, nodes), BF16), split_three(belief), LAST,
+                    preferred_element_type=F32,
+                )
+                mass = mass[:, :groups] + mass[:, groups : 2 * groups] + mass[:, 2 * groups :]
+                mass = jnp.concatenate([mass, jnp.zeros_like(mass)], axis=1)
+                mass_out[round_index] = mass[0:1]
+                mass_in[round_index, me] = mass[0:1]
+
+                @pl.loop(1, n)
+                def _(i):
+                    pltpu.make_async_remote_copy(
+                        src_ref=mass_out.at[round_index], dst_ref=mass_in.at[round_index, me],
+                        send_sem=msend_sem.at[round_index], recv_sem=mrecv_sem.at[round_index],
+                        device_id={"node": lax.rem(me + i, n)},
+                        device_id_type=pl.DeviceIdType.MESH,
+                    ).start()
+
+            if step == 0:
+                lax.fori_loop(0, pairs // TILE, place_pairs, 0)
 
             if late:
                 arrived = mass_in.at[round_index, pl.ds(0, n - 1)]
                 pltpu.make_async_copy(arrived, arrived, mrecv_sem.at[round_index]).wait()
                 mass = loop(
-                    n, lambda b, acc: acc + mass_in[round_index, b], jnp.zeros((8, 2 * cap), F32)
+                    n, lambda b, acc: acc + mass_in[round_index, b], jnp.zeros((1, 2 * cap), F32)
                 )
                 shift = jnp.sum(aff * mass[0:1, :groups], axis=1, keepdims=True) / every_node
                 node_base = base - shift
@@ -276,45 +305,39 @@
 
             acc = loop(pairs // width, local_part, zero)
 
-            arrived = rbuf.at[step, pl.ds(0, n - 1)]
-            pltpu.make_async_copy(arrived, arrived, recv_sem.at[step]).wait()
-
-            def take_part(c, acc):
-                cols = pl.ds(pl.multiple_of(c * width, width), width)
+            final = step == ROUNDS * SWEEPS - 1
+            if final:
+                out_ref[...] = jnp.zeros_like(out_ref)
+                lax.fori_loop(planes, planes + pairs // TILE, back_first, 0)
+                lax.fori_loop(0, pairs // TILE, back_partner, 0)
+
+            def take_part(offset, acc, blocks=group):
+                c = lax.rem(plane - offset + planes, planes)
+                arrived = rbuf.at[step, pl.ds(0, blocks)]
+                pltpu.make_async_copy(arrived, arrived, recv_sem.at[step, c]).wait()
+                cols = pl.ds(pl.multiple_of(c * TILE, TILE), TILE)
                 tiles = []
-                for j in range(width // (2 * cap)):
-                    peer = c * (width // cap) + 2 * j
+                for j in range(group // 2):
+                    peer = c * group + 2 * j
                     b0, b1 = rbuf[step, peer], rbuf[step, peer + 1]
                     top = jnp.where(half, b0, pltpu.roll(b1, cap, 1))
                     low = jnp.where(half, pltpu.roll(b0, cap, 1), b1)
                     tiles.append(jnp.concatenate([top, low], axis=0))
                 fresh = renew(cols, jnp.concatenate(tiles, axis=1))
                 cav[:, cols] = fresh
+                if final:
+                    back_first(c, 0)
                 return add_up(acc, cols, fresh)
 
-            totals = join_three(loop(places // width, take_part, acc))
+            acc = take_part(0, acc, group - 1)
+            if planes <= 4:
+                for k in far_first[-2::-1]:
+                    acc = take_part(k, acc)
+            else:
+                acc = lax.fori_loop(1, planes, take_part, acc)
+            totals = join_three(acc)
 
     marg_ref[...] = softmax_groups(node_base + totals)
-
-    out_ref[...] = jnp.zeros_like(out_ref)
-
-    def back_first(c, _):
-        start = pl.multiple_of(c * TILE, TILE)
-        terms = split_three(cav[:, pl.ds(start, TILE)])
-        out_ref[...] += join_three(jnp.dot(terms, to_slot(start), preferred_element_type=F32))
-        return 0
-
-    lax.fori_loop(0, (places + pairs) // TILE, back_first, 0)
-
-    def back_partner(c, _):
-        start = pl.multiple_of(places + pairs + c * TILE, TILE)
-        terms = split_three(cav[:, pl.ds(start, TILE)])
-        out_ref[...] += join_three(
-            lax.dot_general(terms, from_partner(c), LAST, preferred_element_type=F32)
-        )
-        return 0
-
-    lax.fori_loop(0, pairs // TILE, back_partner, 0)
 
     for step in range(ROUNDS * SWEEPS):
         sent = sbuf.at[step, pl.ds(0, n - 1)]
@@ -351,10 +374,10 @@
             pltpu.VMEM((8, slots // 2), jnp.int32),
             pltpu.VMEM((steps, n, groups // 2, 2 * cap), F32),
             pltpu.VMEM((steps, n, groups // 2, 2 * cap), F32),
-            pltpu.VMEM((ROUNDS, 8, 2 * cap), F32),
-            pltpu.VMEM((ROUNDS, n, 8, 2 * cap), F32),
+            pltpu.VMEM((ROUNDS, 1, 2 * cap), F32),
+            pltpu.VMEM((ROUNDS, n, 1, 2 * cap), F32),
             pltpu.SemaphoreType.DMA((steps,)),
-            pltpu.SemaphoreType.DMA((steps,)),
+            pltpu.SemaphoreType.DMA((steps, places // TILE)),
             pltpu.SemaphoreType.DMA((ROUNDS,)),
             pltpu.SemaphoreType.DMA((ROUNDS,)),
         ],
@@ -365,7 +388,7 @@
         node_field,
         first_messages,
         affinity,
-        group_share.reshape(groups, 1),
+        group_share.reshape(1, groups),
         dst_node.reshape(1, slots),
         send_slots.reshape(1, places),
         send_slots.reshape(n, cap),

time: 61.3 us -> 56.1 us (0.915)
  Pallas kernels: 55.4 us -> 49 us
  local copies, waits for them, and re-layouts: 4.82 us -> 6.08 us
    pallas_call x1, Pallas kernels: 55.4 us -> 49 us  [on_device(): pl.pallas_call(functools.partial(kernel, n), out_shape=(jax.ShapeDtypeStr...]
    unnamed x14 -> x16, local copies, waits for them, and re-layouts: 3.98 us -> 6.02 us
    reshape x1 -> x0, local copies, waits for them, and re-layouts: 0.77 us -> none  [on_device(): group_share.reshape(groups, 1)]
where the time goes in v2:
time: 56.1 us; the launch traced here: 55.7 us
  Pallas kernels  49 us (87%)
  local copies, waits for them, and re-layouts  6.08 us (11%)
  between operations  0.66 us (1%)
    pallas_call x1, Pallas kernels, on_device(): pl.pallas_call(functools.partial(kernel, n), out_shape=(jax.ShapeDtypeStr...  49 us
    unnamed x16, local copies, waits for them, and re-layouts  6.02 us

profile of v2, /device:TPU:0, one launch (start us, length us, event | category | flops | bytes accessed | tf_op | source)
XLA Modules:
  0.0 55.7 jit_solution(15166334089620561128)
XLA Ops:
  0.6 0.0 copy-start.3
  0.6 0.0 copy-start.4
  0.7 0.7 %copy-done.3 = s32[1024]{0:T(1024)S(1)} copy-done((s32[1024]{0:T(1024)S(1)}, s32[1024]{0:T(1024)}, u32[]{:S(2)}) %copy-start.3) | copy-done | bytes 4120
  1.3 0.0 copy-start.6
  1.3 0.1 reshape.22.own_ref
  1.4 0.0 copy-done.4
  1.4 0.6 %copy-done.6 = f32[64]{0:T(128)S(1)} copy-done((f32[64]{0:T(128)S(1)}, f32[64]{0:T(128)}, u32[]{:S(2)}) %copy-start.6) | copy-done | bytes 280
  2.0 0.0 copy-start
  2.0 1.0 %copy-done = f32[64,2048]{1,0:T(8,128)S(1)} copy-done((f32[64,2048]{1,0:T(8,128)S(1)}, f32[64,2048]{1,0:T(8,128)}, u32[]{:S(2)}) %copy-start) | copy-done | bytes 524312
  3.0 0.0 copy-start.1
  3.0 0.8 %copy-done.1 = f32[64,256]{1,0:T(8,128)S(1)} copy-done((f32[64,256]{1,0:T(8,128)S(1)}, f32[64,256]{1,0:T(8,128)}, u32[]{:S(2)}) %copy-start.1) | copy-done | bytes 65560
  3.9 0.0 copy-start.2
  3.9 0.8 %copy-done.2 = f32[64,64]{1,0:T(8,128)S(1)} copy-done((f32[64,64]{1,0:T(8,128)S(1)}, f32[64,64]{1,0:T(8,128)}, u32[]{:S(2)}) %copy-start.2) | copy-done | bytes 16408
  4.6 0.0 copy-start.5
  4.6 0.7 %copy-done.5 = s32[2048]{0:T(1024)S(1)} copy-done((s32[2048]{0:T(1024)S(1)}, s32[2048]{0:T(1024)}, u32[]{:S(2)}) %copy-start.5) | copy-done | bytes 8216
  5.3 49.0 %shard_map.86 = (f32[64,256]{1,0:T(8,128)S(1)}, f32[64,2048]{1,0:T(8,128)S(1)}) custom-call(f32[64,256]{1,0:T(8,128)S(1)} %copy-done.1, f32[64,2048]{1,0:T(8,128)S(1)} %copy-done, f32[64,64]{1,0:T(8,128)S(1)} %copy-done.2, f32[1,64]{1,0:T(1,128)S(1)} %bitcast.7, s32[1,2048]{1,0:T(1,128)S(1)} %bitcast.5, s32[1,1024]{1,0:T(1,128)S(1)} %bitcast.4, ...), custom_call_target="tpu_custom_call" | custom-call | tf_op jit(solution)/shard_map/pallas_call | solution.py:359
  54.3 0.6 %copy.11 = f32[64,256]{1,0:T(8,128)} copy(f32[64,256]{1,0:T(8,128)S(1)} %get-tuple-element.4) | data formatting | bytes 131072
  55.0 0.8 %copy.12 = f32[64,2048]{1,0:T(8,128)} copy(f32[64,2048]{1,0:T(8,128)S(1)} %get-tuple-element.5) | data formatting | bytes 1048576
Async XLA Ops:
  0.6 0.7 %copy-start.3 = (s32[1024]{0:T(1024)S(1)}, s32[1024]{0:T(1024)}, u32[]{:S(2)}) copy-start(s32[1024]{0:T(1024)} %param.12) | copy-start | bytes 12292
  0.6 0.8 %copy-start.4 = (s32[2048]{0:T(1024)S(1)}, s32[2048]{0:T(1024)}, u32[]{:S(2)}) copy-start(s32[2048]{0:T(1024)} %param.11) | copy-start | bytes 24580
  1.3 0.7 %copy-start.6 = (f32[64]{0:T(128)S(1)}, f32[64]{0:T(128)}, u32[]{:S(2)}) copy-start(f32[64]{0:T(128)} %param.10) | copy-start | bytes 772
  2.0 1.0 %copy-start = (f32[64,2048]{1,0:T(8,128)S(1)}, f32[64,2048]{1,0:T(8,128)}, u32[]{:S(2)}) copy-start(f32[64,2048]{1,0:T(8,128)} %first_ref.1) | copy-start | bytes 1572868
  3.0 0.8 %copy-start.1 = (f32[64,256]{1,0:T(8,128)S(1)}, f32[64,256]{1,0:T(8,128)}, u32[]{:S(2)}) copy-start(f32[64,256]{1,0:T(8,128)} %field_ref.1) | copy-start | bytes 196612
  3.9 0.8 %copy-start.2 = (f32[64,64]{1,0:T(8,128)S(1)}, f32[64,64]{1,0:T(8,128)}, u32[]{:S(2)}) copy-start(f32[64,64]{1,0:T(8,128)} %aff_ref.1) | copy-start | bytes 49156
  4.6 0.7 %copy-start.5 = (s32[2048]{0:T(1024)S(1)}, s32[2048]{0:T(1024)}, u32[]{:S(2)}) copy-start(s32[2048]{0:T(1024)} %param.13) | copy-start | bytes 24580

commit v3 on v2

--- a/solution.py
+++ b/solution.py
@@ -211,6 +211,28 @@
         for sweep_index in range(SWEEPS):
             step = round_index * SWEEPS + sweep_index
             late = sweep_index == 0
+            def send_mass():
+                belief = softmax_groups(base + totals)
+                mass = lax.dot_general(
+                    jnp.ones((8, nodes), BF16), split_three(belief), LAST,
+                    preferred_element_type=F32,
+                )
+                mass = mass[:, :groups] + mass[:, groups : 2 * groups] + mass[:, 2 * groups :]
+                mass = jnp.concatenate([mass, jnp.zeros_like(mass)], axis=1)
+                mass_out[round_index] = mass[0:1]
+                mass_in[round_index, me] = mass[0:1]
+
+                @pl.loop(1, n)
+                def _(i):
+                    pltpu.make_async_remote_copy(
+                        src_ref=mass_out.at[round_index], dst_ref=mass_in.at[round_index, me],
+                        send_sem=msend_sem.at[round_index], recv_sem=mrecv_sem.at[round_index],
+                        device_id={"node": lax.rem(me + i, n)},
+                        device_id_type=pl.DeviceIdType.MESH,
+                    ).start()
+
+            if late and step > 0:
+                send_mass()
             logit = (base if late else node_base) + totals
             logit = split_three(logit - jnp.max(logit, axis=0, keepdims=True))
 
@@ -253,27 +275,8 @@
                     lambda k, x: send_part(lax.rem(plane + planes // 2 + k, planes), x), 0,
                 )
 
-            if late:
-                belief = softmax_groups(base + totals)
-                mass = lax.dot_general(
-                    jnp.ones((8, nodes), BF16), split_three(belief), LAST,
-                    preferred_element_type=F32,
-                )
-                mass = mass[:, :groups] + mass[:, groups : 2 * groups] + mass[:, 2 * groups :]
-                mass = jnp.concatenate([mass, jnp.zeros_like(mass)], axis=1)
-                mass_out[round_index] = mass[0:1]
-                mass_in[round_index, me] = mass[0:1]
-
-                @pl.loop(1, n)
-                def _(i):
-                    pltpu.make_async_remote_copy(
-                        src_ref=mass_out.at[round_index], dst_ref=mass_in.at[round_index, me],
-                        send_sem=msend_sem.at[round_index], recv_sem=mrecv_sem.at[round_index],
-                        device_id={"node": lax.rem(me + i, n)},
-                        device_id_type=pl.DeviceIdType.MESH,
-                    ).start()
-
             if step == 0:
+                send_mass()
                 lax.fori_loop(0, pairs // TILE, place_pairs, 0)
 
             if late:

time: 56.1 us -> 52.9 us (0.943)
  Pallas kernels: 49 us -> 45.8 us
    pallas_call x1, Pallas kernels: 49 us -> 45.8 us  [on_device(): pl.pallas_call(functools.partial(kernel, n), out_shape=(jax.ShapeDtypeStr...]
where the time goes in v3:
time: 52.9 us; the launch traced here: 52.5 us
  Pallas kernels  45.8 us (87%)
  local copies, waits for them, and re-layouts  6.08 us (11%)
  between operations  0.66 us (1%)
    pallas_call x1, Pallas kernels, on_device(): pl.pallas_call(functools.partial(kernel, n), out_shape=(jax.ShapeDtypeStr...  45.8 us
    unnamed x16, local copies, waits for them, and re-layouts  6.02 us

profile of v3, /device:TPU:0, one launch (start us, length us, event | category | flops | bytes accessed | tf_op | source)
XLA Modules:
  0.0 52.5 jit_solution(14806174393577145373)
XLA Ops:
  0.6 0.0 copy-start.3
  0.6 0.0 copy-start.4
  0.7 0.7 %copy-done.3 = s32[1024]{0:T(1024)S(1)} copy-done((s32[1024]{0:T(1024)S(1)}, s32[1024]{0:T(1024)}, u32[]{:S(2)}) %copy-start.3) | copy-done | bytes 4120
  1.3 0.0 copy-start.6
  1.3 0.1 reshape.22.own_ref
  1.4 0.0 copy-done.4
  1.4 0.6 %copy-done.6 = f32[64]{0:T(128)S(1)} copy-done((f32[64]{0:T(128)S(1)}, f32[64]{0:T(128)}, u32[]{:S(2)}) %copy-start.6) | copy-done | bytes 280
  2.0 0.0 copy-start
  2.0 1.0 %copy-done = f32[64,2048]{1,0:T(8,128)S(1)} copy-done((f32[64,2048]{1,0:T(8,128)S(1)}, f32[64,2048]{1,0:T(8,128)}, u32[]{:S(2)}) %copy-start) | copy-done | bytes 524312
  3.0 0.0 copy-start.1
  3.0 0.8 %copy-done.1 = f32[64,256]{1,0:T(8,128)S(1)} copy-done((f32[64,256]{1,0:T(8,128)S(1)}, f32[64,256]{1,0:T(8,128)}, u32[]{:S(2)}) %copy-start.1) | copy-done | bytes 65560
  3.9 0.0 copy-start.2
  3.9 0.8 %copy-done.2 = f32[64,64]{1,0:T(8,128)S(1)} copy-done((f32[64,64]{1,0:T(8,128)S(1)}, f32[64,64]{1,0:T(8,128)}, u32[]{:S(2)}) %copy-start.2) | copy-done | bytes 16408
  4.6 0.0 copy-start.5
  4.6 0.7 %copy-done.5 = s32[2048]{0:T(1024)S(1)} copy-done((s32[2048]{0:T(1024)S(1)}, s32[2048]{0:T(1024)}, u32[]{:S(2)}) %copy-start.5) | copy-done | bytes 8216
  5.3 45.8 %shard_map.86 = (f32[64,256]{1,0:T(8,128)S(1)}, f32[64,2048]{1,0:T(8,128)S(1)}) custom-call(f32[64,256]{1,0:T(8,128)S(1)} %copy-done.1, f32[64,2048]{1,0:T(8,128)S(1)} %copy-done, f32[64,64]{1,0:T(8,128)S(1)} %copy-done.2, f32[1,64]{1,0:T(1,128)S(1)} %bitcast.7, s32[1,2048]{1,0:T(1,128)S(1)} %bitcast.5, s32[1,1024]{1,0:T(1,128)S(1)} %bitcast.4, ...), custom_call_target="tpu_custom_call" | custom-call | tf_op jit(solution)/shard_map/pallas_call | solution.py:362
  51.1 0.6 %copy.11 = f32[64,256]{1,0:T(8,128)} copy(f32[64,256]{1,0:T(8,128)S(1)} %get-tuple-element.4) | data formatting | bytes 131072
  51.7 0.8 %copy.12 = f32[64,2048]{1,0:T(8,128)} copy(f32[64,2048]{1,0:T(8,128)S(1)} %get-tuple-element.5) | data formatting | bytes 1048576
Async XLA Ops:
  0.6 0.7 %copy-start.3 = (s32[1024]{0:T(1024)S(1)}, s32[1024]{0:T(1024)}, u32[]{:S(2)}) copy-start(s32[1024]{0:T(1024)} %param.12) | copy-start | bytes 12292
  0.6 0.8 %copy-start.4 = (s32[2048]{0:T(1024)S(1)}, s32[2048]{0:T(1024)}, u32[]{:S(2)}) copy-start(s32[2048]{0:T(1024)} %param.11) | copy-start | bytes 24580
  1.3 0.7 %copy-start.6 = (f32[64]{0:T(128)S(1)}, f32[64]{0:T(128)}, u32[]{:S(2)}) copy-start(f32[64]{0:T(128)} %param.10) | copy-start | bytes 772
  2.0 1.0 %copy-start = (f32[64,2048]{1,0:T(8,128)S(1)}, f32[64,2048]{1,0:T(8,128)}, u32[]{:S(2)}) copy-start(f32[64,2048]{1,0:T(8,128)} %first_ref.1) | copy-start | bytes 1572868
  3.0 0.8 %copy-start.1 = (f32[64,256]{1,0:T(8,128)S(1)}, f32[64,256]{1,0:T(8,128)}, u32[]{:S(2)}) copy-start(f32[64,256]{1,0:T(8,128)} %field_ref.1) | copy-start | bytes 196612
  3.9 0.8 %copy-start.2 = (f32[64,64]{1,0:T(8,128)S(1)}, f32[64,64]{1,0:T(8,128)}, u32[]{:S(2)}) copy-start(f32[64,64]{1,0:T(8,128)} %aff_ref.1) | copy-start | bytes 49156
  4.6 0.7 %copy-start.5 = (s32[2048]{0:T(1024)S(1)}, s32[2048]{0:T(1024)}, u32[]{:S(2)}) copy-start(s32[2048]{0:T(1024)} %param.13) | copy-start | bytes 24580
